TPU v7x, 32 devices: a whole 2x2x4 slice. The times are simulated.
32 devices in a mesh: grp: 2 (over core), fsdp: 16 (over z, y, x).
Axes of the slice: x: 2, y: 2, z: 4, core: 2. Of those that a mesh axis runs over, the one named last changes fastest.
Arguments:
- scorer_hidden: bfloat16 [4096, 4096], P(('grp', 'fsdp')), may hold values from -6 to 6
- scorer_gain: float32 [4096], replicated, may hold values from 0.3 to 40
- scorer_head: bfloat16 [4096, 65536], P(None, ('grp', 'fsdp')), may hold values from -0.09375 to 0.09375
- targets: int32 [4096], P(('grp', 'fsdp')), may hold values from 0 to 65535
- ranks: int32 [4096], P(('grp', 'fsdp')), may hold values from 0 to 2047, as said below
- train_input: bfloat16 [4096, 8192], P(('grp', 'fsdp')), may hold values from -6 to 6
- cotangent: bfloat16 [4096, 8192], P(('grp', 'fsdp')), may hold values from -6 to 6
- w_gate: bfloat16 [14336, 8192], P('fsdp', 'grp'), may hold values from -0.0625 to 0.0625
- w_up: bfloat16 [14336, 8192], P('fsdp', 'grp'), may hold values from -0.0625 to 0.0625
- w_down: bfloat16 [14336, 8192], P('fsdp', 'grp'), may hold values from -0.046875 to 0.046875
Outputs:
- token_loss: float32 [4096], P(('grp', 'fsdp'))
- grad_gate: bfloat16 [14336, 8192], P('fsdp', 'grp')
- grad_up: bfloat16 [14336, 8192], P('fsdp', 'grp')
- grad_down: bfloat16 [14336, 8192], P('fsdp', 'grp')
Inputs may be any that keep to these rules, and one draw needn't show every extreme that they name: Within each half of the tokens (the first 2048 and the last 2048) the ranks are a permutation of 0 to 2047. The 128 tokens of one device hold at most 2 with rank under 16, and some device holds exactly 2.
All inputs are finite; a program needn't handle non-finite values.
Results may differ from a plain program's by a relative error of at most 0.005.
Values may be sent and summed in bfloat16 or wider, within the bound.
A program may use at most 384 MiB of HBM per device.

v0:
```python
import jax
import jax.numpy as jnp
from jax import lax
from jax.sharding import PartitionSpec as P

CAP = 2


def on_device(
    scorer_hidden,
    scorer_gain,
    scorer_head,
    targets,
    ranks,
    train_input,
    cotangent,
    w_gate,
    w_up,
    w_down,
):
    slot_count = CAP
    shard_count = lax.axis_size("fsdp")
    keep_half = shard_count * slot_count // 2
    own_index = lax.axis_index("grp") * shard_count + lax.axis_index("fsdp")
    chosen = (ranks < keep_half).astype(jnp.int32)
    slot_place = jnp.cumsum(chosen) - 1
    slot_ids = lax.iota(jnp.int32, slot_count)
    picker = (slot_place[None, :] == slot_ids[:, None]) & (chosen[None, :] > 0)
    pick_bf = picker.astype(jnp.bfloat16)
    hidden_rows = jnp.dot(pick_bf, scorer_hidden, preferred_element_type=jnp.float32)
    target_rows = jnp.sum(picker.astype(jnp.int32) * targets[None, :], axis=1)
    mean_square = jnp.mean(hidden_rows * hidden_rows, axis=1, keepdims=True)
    normed = (hidden_rows * lax.rsqrt(mean_square + 1e-05) * scorer_gain[None, :]).astype(
        jnp.bfloat16
    )
    input_rows = jnp.dot(pick_bf, train_input, preferred_element_type=jnp.float32).astype(
        jnp.bfloat16
    )
    cotangent_rows = jnp.dot(pick_bf, cotangent, preferred_element_type=jnp.float32).astype(
        jnp.bfloat16
    )
    score_width = scorer_hidden.shape[1]
    model_width = train_input.shape[1]
    half_width = w_gate.shape[1]
    packed = jnp.concatenate([normed, input_rows, cotangent_rows], axis=1)
    gathered, target_all = (
        lax.all_gather(packed, ("grp", "fsdp"), axis=0, tiled=True),
        lax.all_gather(target_rows, ("grp", "fsdp"), axis=0, tiled=True),
    )
    normed_all = gathered[:, :score_width]
    column = lax.axis_index("grp") * half_width
    inputs = lax.dynamic_slice_in_dim(gathered, score_width + column, half_width, axis=1)
    upstream = lax.dynamic_slice_in_dim(
        gathered, score_width + model_width + column, half_width, axis=1
    )

    def part(rows, weights):
        return jnp.einsum("sd,fd->sf", rows, weights, preferred_element_type=jnp.float32)

    parts = jnp.concatenate(
        [part(inputs, w_gate), part(inputs, w_up), part(upstream, w_down)], axis=1
    )
    gate, up_part, dhidden = jnp.split(lax.psum(parts, "grp"), 3, axis=1)
    logits = jnp.dot(normed_all, scorer_head, preferred_element_type=jnp.float32)
    vocab_width = scorer_head.shape[1]
    vocab_start = own_index * vocab_width
    target_hit = target_all[:, None] - vocab_start == lax.iota(jnp.int32, vocab_width)[None, :]
    highest = jnp.max(logits, axis=1)
    target_logit = jnp.sum(jnp.where(target_hit, logits, 0.0), axis=1)
    rescaled = jnp.sum(jnp.exp(logits - highest[:, None]), axis=1)
    stats = lax.all_gather(jnp.stack([highest, rescaled, target_logit]), ("grp", "fsdp"), axis=0)
    own = lax.dynamic_slice_in_dim(stats, own_index * slot_count, slot_count, axis=2)
    peak = jnp.max(own[:, 0], axis=0)
    total = jnp.sum(own[:, 1] * jnp.exp(own[:, 0] - peak[None, :]), axis=0)
    own_losses = peak + jnp.log(total) - jnp.sum(own[:, 2], axis=0)
    token_loss = jnp.sum(picker.astype(jnp.float32) * own_losses[:, None], axis=0)
    sigmoid_gate = jax.nn.sigmoid(gate)
    act = gate * sigmoid_gate
    hidden = (act * up_part).astype(jnp.bfloat16)
    dgate = (dhidden * up_part * sigmoid_gate * (1.0 + gate * (1.0 - sigmoid_gate))).astype(
        jnp.bfloat16
    )
    dup = (dhidden * act).astype(jnp.bfloat16)

    def outer(left, right):
        return jnp.einsum("sf,sd->fd", left, right, preferred_element_type=jnp.float32).astype(
            jnp.bfloat16
        )

    return token_loss, outer(dgate, inputs), outer(dup, inputs), outer(hidden, upstream)


def solution(mesh):
    in_specs = (
        P(("grp", "fsdp"), None),
        P(),
        P(None, ("grp", "fsdp")),
        P(("grp", "fsdp")),
        P(("grp", "fsdp")),
        P(("grp", "fsdp"), None),
        P(("grp", "fsdp"), None),
        P("fsdp", "grp"),
        P("fsdp", "grp"),
        P("fsdp", "grp"),
    )
    out_specs = (P(("grp", "fsdp")), P("fsdp", "grp"), P("fsdp", "grp"), P("fsdp", "grp"))
    return jax.shard_map(
        on_device, mesh=mesh, in_specs=in_specs, out_specs=out_specs, check_vma=False
    )
```

profile of v0, /device:TPU:0, one launch (start us, length us, event | category | flops | bytes accessed | tf_op | source)
XLA Modules:
  0.0 199.2 jit_solution(15563625370113163632)
XLA Ops:
  7.2 0.0 copy-start
  7.2 0.0 all-gather.5.cloned.1.call-start
  7.2 0.8 fusion.25
  8.0 0.1 copy.23
  8.1 0.2 reduce-window.8
  8.3 0.1 add_reduce_fusion
  8.4 0.8 select_reduce_fusion.2
  9.2 0.0 copy-done
  9.2 0.4 convolution_convert_fusion
  9.6 2.0 convolution_convert_fusion.1
  11.6 1.6 multiply_reduce_fusion
  13.2 0.8 multiply_convert_fusion.6
  14.0 0.7 maximum_bitcast_fusion
  14.7 0.0 all-gather.5.cloned.1.call-update
  14.7 0.0 all-reduce.3.cloned.1.call-start
  14.8 0.2 dynamic-update-slice
  15.0 42.0 %all-reduce = s32[64]{0:T(128)S(1)} all-reduce(s32[64]{0:T(128)S(1)} %dynamic-update-slice), channel_id=1, replica_groups=mesh['grp'=2,'fsdp'=16] {'grp','fsdp'}, use_global_device_ids=true, to_apply=%add | all-reduce | flops 64 | bytes 512
  57.1 18.6 %all-gather.5.cloned.1.call-done = bf16[32,2,20480]{2,1,0:T(2,128)(2,1)} async-done(((bf16[1,2,20480]{2,1,0:T(2,128)(2,1)}), bf16[32,2,20480]{2,1,0:T(2,128)(2,1)}) %all-gather.5.cloned.1.call-update) | async-done | bytes 2621456 | tf_op jit(solution)/shard_map/all_gather | solution.py:47
  75.6 4.4 %reshape.65 = bf16[64,20480]{1,0:T(8,128)(2,1)} reshape(bf16[32,2,20480]{2,1,0:T(2,128)(2,1)} %all-gather.5.cloned.1.call-done) | data formatting | bytes 5242880
  80.0 0.0 slice-start
  80.0 5.7 %fusion.7 = f32[64,896]{1,0:T(8,128)S(1)} fusion(bf16[896,4096]{1,0:T(8,128)(2,1)} %param.18, bf16[64,20480]{1,0:T(8,128)(2,1)} %reshape.65, s32[]{:T(128)S(6)} %select_n.15), kind=kOutput, calls=%fused_computation.16 | convolution fusion | flops 469762048 | bytes 8093700 | tf_op jit(solution)/shard_map/sd,fd->sf/dot_general | solution.py:58
  85.8 0.0 slice-start.1
  85.8 5.7 %fusion.9 = f32[64,896]{1,0:T(8,128)S(1)} fusion(bf16[896,4096]{1,0:T(8,128)(2,1)} %param.17, bf16[64,20480]{1,0:T(8,128)(2,1)} %reshape.65, s32[]{:T(128)S(6)} %select_n.15), kind=kOutput, calls=%fused_computation.18 | convolution fusion | flops 469762048 | bytes 8093700 | tf_op jit(solution)/shard_map/sd,fd->sf/dot_general | solution.py:58
  91.5 0.0 slice-done
  91.5 0.0 slice-done.1
  91.6 3.4 %fusion.3 = f32[64,896]{1,0:T(8,128)S(1)} fusion(bf16[896,4096]{1,0:T(8,128)(2,1)S(1)} %bitcast.30, bf16[64,20480]{1,0:T(8,128)(2,1)} %reshape.65, s32[]{:T(128)S(6)} %select_n.16), kind=kOutput, calls=%fused_computation.12 | convolution fusion | flops 469762048 | bytes 8093700 | tf_op jit(solution)/shard_map/sd,fd->sf/dot_general | solution.py:58
  95.0 0.9 pad_maximum_fusion
  95.9 0.0 all-reduce.3.cloned.1.call-update
  95.9 9.3 %fusion.30 = (f32[64]{0:T(128)S(1)}, f32[64,2048]{1,0:T(8,128)S(1)}) fusion(bf16[4096,2048]{1,0:T(8,128)(2,1)} %param.12, bf16[64,20480]{1,0:T(8,128)(2,1)} %reshape.65), kind=kOutput, calls=%fused_computation.57 | convolution fusion | flops 1073872896 | bytes 17826048 | tf_op jit(solution)/shard_map/dot_general | solution.py:64
  105.2 0.3 exponential_reduce_fusion
  105.5 66.6 %all-gather.2 = f32[32,3,64]{2,1,0:T(4,128)S(1)} all-gather(f32[1,3,64]{2,1,0:T(4,128)S(1)} %maximum_bitcast_fusion.1), channel_id=2, replica_groups=mesh['grp'=2,'fsdp'=16] {'grp','fsdp'}, dimensions={0}, use_global_device_ids=true | all-gather | bytes 25344 | tf_op jit(solution)/shard_map/all_gather | solution.py:71
  172.1 0.2 fusion.29
  172.3 0.1 copy.25
  172.3 0.1 copy.24
  172.4 0.2 fusion.23
  172.6 0.6 select_reduce_fusion.1
  173.2 0.0 all-reduce.3.cloned.1.call-done
  173.2 0.0 copy-start.2
  173.2 6.5 %convolution_convert_fusion.2 = bf16[896,4096]{1,0:T(8,128)(2,1)} fusion(bf16[64,20480]{1,0:T(8,128)(2,1)} %reshape.65, s32[]{:T(128)S(6)} %select_n.16, f32[64,2688]{1,0:T(8,128)} %all-reduce.3.cloned.1.call-done), kind=kOutput, calls=%fused_computation.2 | convolution fusion | flops 473776128 | bytes 8323076 | tf_op jit(solution)/shard_map/sf,sd->fd/dot_general | solution.py:86
  179.7 0.0 copy-done.2
  179.7 0.0 copy-start.1
  179.7 6.4 %convolution_convert_fusion.4 = bf16[896,4096]{1,0:T(8,128)(2,1)} fusion(bf16[64,20480]{1,0:T(8,128)(2,1)} %reshape.65, s32[]{:T(128)S(6)} %select_n.15, f32[64,2688]{1,0:T(8,128)S(1)} %copy-done.2), kind=kOutput, calls=%fused_computation.4 | convolution fusion | flops 474005504 | bytes 8552452 | tf_op jit(solution)/shard_map/sf,sd->fd/dot_general | solution.py:86
  186.1 6.2 %convolution_convert_fusion.3 = bf16[896,4096]{1,0:T(8,128)(2,1)} fusion(bf16[64,20480]{1,0:T(8,128)(2,1)} %reshape.65, s32[]{:T(128)S(6)} %select_n.15, f32[64,2688]{1,0:T(8,128)S(1)} %copy-done.2), kind=kOutput, calls=%fused_computation.3 | convolution fusion | flops 473776128 | bytes 8323076 | tf_op jit(solution)/shard_map/sf,sd->fd/dot_general | solution.py:86
  192.3 0.0 copy-done.1
  (6 shorter events, 0.0 us)
Async XLA Ops:
  7.2 2.0 %copy-start = (bf16[128,8192]{1,0:T(8,128)(2,1)S(1)}, bf16[128,8192]{1,0:T(8,128)(2,1)}, u32[]{:S(2)}) copy-start(bf16[128,8192]{1,0:T(8,128)(2,1)} %param.16) | copy-start | bytes 6291460
  7.2 68.4 %all-gather.5.cloned.1.call-start = ((), (), s32[]{:S(2)}) async-start(), calls=%async_computation.1 | async-start | bytes 2703360 | tf_op jit(solution)/shard_map/all_gather | solution.py:47
  14.7 158.5 %all-reduce.3.cloned.1.call-start = ((), (), s32[]{:S(2)}) async-start(), calls=%async_computation | async-start | bytes 1376256 | tf_op jit(solution)/shard_map/psum | solution.py:63
  80.0 11.5 %slice-start = ((s8[7340032]{0:T(1024)(128)(4,1)}), s8[4194304]{0:T(1024)(128)(4,1)S(1)}, s32[]{:S(2)}) async-start(s8[7340032]{0:T(1024)(128)(4,1)} %bitcast.29), calls=%async_computation.2 | async-start | bytes 8388608
  85.8 5.8 %slice-start.1 = ((s8[7340032]{0:T(1024)(128)(4,1)}), s8[3145728]{0:T(1024)(128)(4,1)S(1)}, s32[]{:S(2)}) async-start(s8[7340032]{0:T(1024)(128)(4,1)} %bitcast.29), calls=%async_computation.3 | async-start | bytes 6291456
  173.2 6.5 %copy-start.2 = (f32[64,2688]{1,0:T(8,128)S(1)}, f32[64,2688]{1,0:T(8,128)}, u32[]{:S(2)}) copy-start(f32[64,2688]{1,0:T(8,128)} %all-reduce.3.cloned.1.call-done) | copy-start | bytes 2064388
  179.7 12.6 %copy-start.1 = (bf16[128,8192]{1,0:T(8,128)(2,1)S(1)}, bf16[128,8192]{1,0:T(8,128)(2,1)}, u32[]{:S(2)}) copy-start(bf16[128,8192]{1,0:T(8,128)(2,1)} %param.16) | copy-start | bytes 6291460
Sparse Core Ops, SparseCore 0:
  14.8 60.7 all-gather.4
  96.0 17.9 all-reduce.2
where the time goes:
time: 200 us; the launch traced here: 199 us
  blocking collectives  109 us (54%)
  matrix products  47.2 us (24%)
  waiting for transfers between devices  18.6 us (9%)
  between operations  14.2 us (7%)
  other arithmetic  5.58 us (3%)
  local copies, waits for them, and re-layouts  4.93 us (2%)
    all_gather x1, blocking collectives, on_device(): lax.all_gather(jnp.stack([highest, rescaled, target_logit]), ('grp', 'fsd...  66.6 us
    unnamed x1, blocking collectives  42 us
    dot_general x3, matrix products, outer(): jnp.einsum('sf,sd->fd', left, right, preferred_element_type=jnp.float32)  19.1 us
    all_gather x1, waiting for transfers between devices, on_device(): lax.all_gather(packed, ('grp', 'fsdp'), axis=0, tiled=True)  18.6 us
    dot_general x3, matrix products, part(): jnp.einsum('sd,fd->sf', rows, weights, preferred_element_type=jnp.float32)  14.9 us
    dot_general x1, matrix products, on_device(): jnp.dot(normed_all, scorer_head, preferred_element_type=jnp.float32)  9.3 us
    unnamed x13, local copies, waits for them, and re-layouts  4.66 us
  transfers between devices with their start and end apart: 2, of which 1 were waited for; matrix products, arithmetic and copies ran while one was open for 6% of the time, Pallas kernels for 0%

commit v1 on v0

v1 whole, which is shorter than its diff:
```python
import functools

import jax
import jax.numpy as jnp
from jax import lax
from jax.experimental import pallas as pl
from jax.experimental.pallas import tpu as pltpu
from jax.sharding import PartitionSpec as P

CAP = 2
SLOTS = 2 * CAP
QUARTERS = 4
ROWS = SLOTS * QUARTERS
F32 = jnp.float32
BF16 = jnp.bfloat16
MESH = pl.DeviceIdType.MESH


def exchange_kernel(
    n,
    gain_ref,
    targets_ref,
    ranks_ref,
    hidden_hbm,
    input_hbm,
    cot_hbm,
    gate_hbm,
    up_hbm,
    down_hbm,
    head_hbm,
    loss_ref,
    left_ref,
    x_ref,
    u_ref,
    hidden_v,
    input_v,
    cot_v,
    weight_v,
    head_v,
    block_v,
    mate_v,
    gather_v,
    normed_v,
    part_v,
    other_v,
    logits_v,
    stat_v,
    stat_in,
    load_sem,
    send_sem,
    mate_sem,
    gather_sem,
    normed_sem,
    part_sem,
    stat_sem,
):
    groups = n // 4
    slots = n * SLOTS
    core = lax.axis_index("grp")
    chip = lax.axis_index("fsdp")
    a, b, c = chip // 4, lax.rem(chip // 2, 2), lax.rem(chip, 2)

    def at(a_, b_, c_):
        return a_ * 4 + b_ * 2 + c_

    mate = (1 - core, chip)
    y_peer = (core, at(a, 1 - b, c))
    x_peer = (core, at(a, b, 1 - c))
    z_to = [(core, at(lax.rem(a + d, groups), b, c)) for d in range(1, groups)]
    peers = [mate, y_peer, x_peer] + z_to

    loads = [
        pltpu.make_async_copy(src, dst, load_sem.at[i])
        for i, (src, dst) in enumerate(
            [
                (hidden_hbm, hidden_v),
                (input_hbm, input_v),
                (cot_hbm, cot_v),
                (gate_hbm, weight_v.at[0]),
                (up_hbm, weight_v.at[1]),
                (down_hbm, weight_v.at[2]),
                (head_hbm, head_v),
            ]
        )
    ]
    for load in loads:
        load.start()

    barrier = pltpu.get_barrier_semaphore()
    for peer in peers:
        pl.semaphore_signal(barrier, inc=1, device_id=peer, device_id_type=MESH)

    sends = []

    def send(src, dst, recv_sem, peer):
        copy = pltpu.make_async_remote_copy(
            src_ref=src,
            dst_ref=dst,
            send_sem=send_sem.at[len(sends)],
            recv_sem=recv_sem,
            device_id=peer,
            device_id_type=MESH,
        )
        copy.start()
        sends.append(copy)

    def arrived(dst, recv_sem, peer):
        pltpu.make_async_remote_copy(
            src_ref=dst,
            dst_ref=dst,
            send_sem=send_sem.at[0],
            recv_sem=recv_sem,
            device_id=peer,
            device_id_type=MESH,
        ).wait_recv()

    tokens = ranks_ref.shape[1]
    half = weight_v.shape[2]
    piece = half // QUARTERS
    score = hidden_v.shape[1]
    score_half = score // 2
    score_piece = score_half // QUARTERS
    keep_half = n * CAP // 2
    chosen = ranks_ref[...] < keep_half
    chosen_rows = jnp.broadcast_to(chosen.astype(F32), (16, tokens)).astype(BF16)
    before = (
        lax.broadcasted_iota(jnp.int32, (tokens, tokens), 0)
        < lax.broadcasted_iota(jnp.int32, (tokens, tokens), 1)
    ).astype(F32).astype(BF16)
    place = jnp.dot(chosen_rows, before, preferred_element_type=F32).astype(jnp.int32)
    row = lax.broadcasted_iota(jnp.int32, (ROWS, tokens), 0)
    row_slot = lax.rem(row, SLOTS) - core * CAP
    picked = (place == row_slot) & (chosen_rows.astype(F32) > 0)
    picks = [
        (picked & (row // SLOTS == q)).astype(F32).astype(BF16) for q in range(QUARTERS)
    ]

    def select(ref, start, width):
        total = None
        for q in range(QUARTERS):
            term = jnp.dot(
                picks[q],
                ref[:, start + q * width : start + (q + 1) * width],
                preferred_element_type=F32,
            )
            total = term if total is None else total + term
        return total

    targets = targets_ref[...]
    first = (picked & (row < SLOTS)).astype(F32)
    high = jnp.sum(first * (targets // 256).astype(F32), axis=1, keepdims=True)
    low = jnp.sum(first * lax.rem(targets, 256).astype(F32), axis=1, keepdims=True)
    lane = lax.broadcasted_iota(jnp.int32, (ROWS, 128), 1)
    digits = jnp.where(lane == 0, high, jnp.where(lane == 1, low, 0.0)).astype(BF16)

    loads[0].wait()
    halves = [select(hidden_v, h * score_half, score_piece) for h in range(2)]
    square = sum(jnp.sum(v * v, axis=1, keepdims=True) for v in halves)
    square = sum(square[q * SLOTS : (q + 1) * SLOTS] for q in range(QUARTERS))
    scale = lax.rsqrt(square / score + 1e-05)
    scale = jnp.concatenate([scale] * QUARTERS, axis=0)
    piece_row = lax.broadcasted_iota(jnp.int32, (ROWS, score_piece), 0) // SLOTS
    tail = 2 * piece
    end = tail + score_piece
    for h in range(2):
        gain = jnp.zeros((ROWS, score_piece), F32)
        for q in range(QUARTERS):
            start = h * score_half + q * score_piece
            gain = jnp.where(piece_row == q, gain_ref[:, start : start + score_piece], gain)
        block_v[h, :, tail:end] = (halves[h] * scale * gain).astype(BF16)
        block_v[h, :, end:] = digits
    loads[1].wait()
    loads[2].wait()
    for h in range(2):
        block_v[h, :, :piece] = select(input_v, h * half, piece).astype(BF16)
        block_v[h, :, piece:tail] = select(cot_v, h * half, piece).astype(BF16)

    pl.semaphore_wait(barrier, len(peers))
    send(block_v.at[1 - core], mate_v, mate_sem.at[0], mate)
    arrived(mate_v, mate_sem.at[0], mate)
    gather_v[chip] = block_v[core] + mate_v[...]

    width = gather_v.shape[2]
    cut = (width // 128 + 1) // 2 * 128
    z_sem, y_sem, x_sem, ya_sem, xb_sem = (gather_sem.at[i] for i in range(5))
    for d in range(1, groups):
        own = gather_v.at[chip]
        send(own, own, z_sem.at[d], z_to[d - 1])
    for d in range(groups):
        source = lax.rem(a + groups - d, groups)
        block = gather_v.at[at(source, b, c)]
        if d:
            arrived(block, z_sem.at[d], (core, at(source, b, c)))
        send(block, block, y_sem.at[d], y_peer)
        send(block, block, x_sem.at[d], x_peer)
    for d in range(groups):
        source = lax.rem(a + groups - d, groups)
        block = gather_v.at[at(source, 1 - b, c)]
        arrived(block, y_sem.at[d], y_peer)
        block = block.at[:, pl.ds(0, cut)]
        send(block, block, xb_sem.at[d], x_peer)
        block = gather_v.at[at(source, b, 1 - c)]
        arrived(block, x_sem.at[d], x_peer)
        block = block.at[:, pl.ds(cut, width - cut)]
        send(block, block, ya_sem.at[d], y_peer)
    for d in range(groups):
        source = lax.rem(a + groups - d, groups)
        block = gather_v.at[at(source, 1 - b, 1 - c)]
        arrived(block.at[:, pl.ds(0, cut)], xb_sem.at[d], x_peer)
        arrived(block.at[:, pl.ds(cut, width - cut)], ya_sem.at[d], y_peer)

    def take(q, start, stop):
        rows = gather_v[:, :, start:stop].reshape(n * ROWS, stop - start)
        slot = lax.broadcasted_iota(jnp.int32, (slots, n * ROWS), 0)
        place = lax.broadcasted_iota(jnp.int32, (slots, n * ROWS), 1)
        wanted = slot // SLOTS * ROWS + q * SLOTS + lax.rem(slot, SLOTS)
        pick = (place == wanted).astype(F32).astype(BF16)
        return jnp.dot(pick, rows, preferred_element_type=F32)

    for q in range(QUARTERS):
        normed_v[core, :, q * score_piece : (q + 1) * score_piece] = take(q, tail, end).astype(
            BF16
        )
    send(normed_v.at[core], normed_v.at[core], normed_sem.at[0], mate)
    digits = take(0, end, width)
    target = (digits[:, 0:1] * 256.0 + digits[:, 1:2]).astype(jnp.int32)
    for q in range(QUARTERS):
        x_ref[:, q * piece : (q + 1) * piece] = take(q, 0, piece).astype(BF16)
        u_ref[:, q * piece : (q + 1) * piece] = take(q, piece, tail).astype(BF16)

    units = weight_v.shape[1]
    tile = units // 2 if units % 256 == 0 else units
    for i, rows in enumerate([x_ref, x_ref, u_ref]):
        loads[3 + i].wait()

        @pl.loop(0, units // tile)
        def _(j):
            at_units = pl.ds(pl.multiple_of(j * tile, tile), tile)
            part_v[i, at_units, :] = lax.dot_general(
                weight_v[i, at_units, :],
                rows[...],
                (((1,), (1,)), ((), ())),
                preferred_element_type=F32,
            )

        send(part_v.at[i], other_v.at[i], part_sem.at[i], mate)

    loads[6].wait()
    arrived(normed_v.at[1 - core], normed_sem.at[0], mate)
    vocab = head_v.shape[1]
    v_tile = 256

    @pl.loop(0, vocab // v_tile)
    def _(j):
        at_vocab = pl.ds(pl.multiple_of(j * v_tile, v_tile), v_tile)
        logits_v[:, at_vocab] = jnp.dot(
            normed_v[0], head_v[:score_half, at_vocab], preferred_element_type=F32
        ) + jnp.dot(normed_v[1], head_v[score_half:, at_vocab], preferred_element_type=F32)

    logits = logits_v[...]
    entry = lax.broadcasted_iota(jnp.int32, (slots, vocab), 1)
    hit = entry == target - (core * n + chip) * vocab
    peak = jnp.max(logits, axis=1, keepdims=True)
    total = jnp.sum(jnp.exp(logits - peak), axis=1, keepdims=True)
    wanted = jnp.sum(jnp.where(hit, logits, 0.0), axis=1, keepdims=True)
    lane = lax.broadcasted_iota(jnp.int32, (slots, 128), 1)

    def pack(stats):
        return jnp.where(lane == 0, stats[0], jnp.where(lane == 1, stats[1], stats[2]))

    def combine(terms):
        peak = functools.reduce(jnp.maximum, [t[0] for t in terms])
        total = sum(t[1] * jnp.exp(t[0] - peak) for t in terms)
        return peak, total, sum(t[2] for t in terms)

    def split(packed):
        return packed[:, 0:1], packed[:, 1:2], packed[:, 2:3]

    stats = (peak, total, wanted)

    def multiply(i):
        arrived(other_v.at[i], part_sem.at[i], mate)
        return part_v[i] + other_v[i]

    for i, peer in enumerate([mate, x_peer, y_peer]):
        stat_v[i] = pack(stats)
        send(stat_v.at[i], stat_in.at[i], stat_sem.at[i], peer)
        if i == 0:
            gate = multiply(0)
            up = multiply(1)
            s = jax.nn.sigmoid(gate)
            act = gate * s
            left_ref[2] = (act * up).astype(BF16)
            dhidden = multiply(2)
            left_ref[0] = (dhidden * up * s * (1.0 + gate * (1.0 - s))).astype(BF16)
            left_ref[1] = (dhidden * act).astype(BF16)
        arrived(stat_in.at[i], stat_sem.at[i], peer)
        stats = combine([stats, split(stat_in[i])])
    stat_v[3] = pack(stats)
    for d in range(1, groups):
        send(stat_v.at[3], stat_in.at[2 + d], stat_sem.at[2 + d], z_to[d - 1])
    terms = [stats]
    for d in range(1, groups):
        source = (core, at(lax.rem(a + groups - d, groups), b, c))
        arrived(stat_in.at[2 + d], stat_sem.at[2 + d], source)
        terms.append(split(stat_in[2 + d]))
    peak, total, wanted = combine(terms)
    losses = peak + jnp.log(total) - wanted
    slot = lax.broadcasted_iota(jnp.int32, (slots, tokens), 0)
    mine = slot == place[0:1] + chip * SLOTS + core * CAP
    mine = mine & (jnp.broadcast_to(ranks_ref[...], (slots, tokens)) < keep_half)
    loss_ref[...] = jnp.sum(jnp.where(mine, losses, 0.0), axis=0, keepdims=True)
    for copy in sends:
        copy.wait_send()


def outer_kernel(left_ref, x_ref, u_ref, gate_ref, up_ref, down_ref):
    for i, (right, out) in enumerate([(x_ref, gate_ref), (x_ref, up_ref), (u_ref, down_ref)]):
        width = out.shape[1]
        step = 1024 if width % 1024 == 0 else width
        for k in range(width // step):
            out[:, k * step : (k + 1) * step] = jnp.dot(
                left_ref[i], right[:, k * step : (k + 1) * step], preferred_element_type=F32
            ).astype(BF16)


def on_device(
    scorer_hidden,
    scorer_gain,
    scorer_head,
    targets,
    ranks,
    train_input,
    cotangent,
    w_gate,
    w_up,
    w_down,
):
    n = lax.axis_size("fsdp")
    groups = n // 4
    slots = n * SLOTS
    score, vocab = scorer_head.shape
    units, half = w_gate.shape
    tokens = ranks.shape[0]
    width = 2 * half // QUARTERS + score // 2 // QUARTERS + 128
    vmem = pl.BlockSpec(memory_space=pltpu.VMEM)
    hbm = pl.BlockSpec(memory_space=pl.ANY)
    n_sends = 1 + (groups - 1) + 4 * groups + 1 + 3 + 3 + (groups - 1)
    dma = pltpu.SemaphoreType.DMA
    loss, left, inputs, upstream = pl.pallas_call(
        functools.partial(exchange_kernel, n),
        out_shape=(
            jax.ShapeDtypeStruct((1, tokens), F32),
            jax.ShapeDtypeStruct((3, units, slots), BF16),
            jax.ShapeDtypeStruct((slots, half), BF16),
            jax.ShapeDtypeStruct((slots, half), BF16),
        ),
        in_specs=[vmem] * 3 + [hbm] * 7,
        out_specs=(vmem,) * 4,
        scratch_shapes=[
            pltpu.VMEM(scorer_hidden.shape, BF16),
            pltpu.VMEM(train_input.shape, BF16),
            pltpu.VMEM(cotangent.shape, BF16),
            pltpu.VMEM((3, units, half), BF16),
            pltpu.VMEM((score, vocab), BF16),
            pltpu.VMEM((2, ROWS, width), BF16),
            pltpu.VMEM((ROWS, width), BF16),
            pltpu.VMEM((n, ROWS, width), BF16),
            pltpu.VMEM((2, slots, score // 2), BF16),
            pltpu.VMEM((3, units, slots), F32),
            pltpu.VMEM((3, units, slots), F32),
            pltpu.VMEM((slots, vocab), F32),
            pltpu.VMEM((4, slots, 128), F32),
            pltpu.VMEM((2 + groups, slots, 128), F32),
            dma((7,)),
            dma((n_sends,)),
            dma((1,)),
            dma((5, groups)),
            dma((1,)),
            dma((3,)),
            dma((2 + groups,)),
        ],
        compiler_params=pltpu.CompilerParams(
            collective_id=0, has_side_effects=True, vmem_limit_bytes=60 * 2**20
        ),
    )(
        scorer_gain.reshape(1, score),
        targets.reshape(1, tokens),
        ranks.reshape(1, tokens),
        scorer_hidden,
        train_input,
        cotangent,
        w_gate,
        w_up,
        w_down,
        scorer_head,
    )
    tile = 128 if units % 128 == 0 else units
    whole = pl.BlockSpec((slots, half), lambda i: (0, 0))
    out = pl.BlockSpec((tile, half), lambda i: (i, 0))
    grads = pl.pallas_call(
        outer_kernel,
        grid=(units // tile,),
        out_shape=(jax.ShapeDtypeStruct((units, half), BF16),) * 3,
        in_specs=[pl.BlockSpec((3, tile, slots), lambda i: (0, i, 0)), whole, whole],
        out_specs=(out,) * 3,
        compiler_params=pltpu.CompilerParams(vmem_limit_bytes=48 * 2**20),
    )(left, inputs, upstream)
    return (loss.reshape(tokens),) + tuple(grads)


def solution(mesh):
    in_specs = (
        P(("grp", "fsdp"), None),
        P(),
        P(None, ("grp", "fsdp")),
        P(("grp", "fsdp")),
        P(("grp", "fsdp")),
        P(("grp", "fsdp"), None),
        P(("grp", "fsdp"), None),
        P("fsdp", "grp"),
        P("fsdp", "grp"),
        P("fsdp", "grp"),
    )
    out_specs = (P(("grp", "fsdp")), P("fsdp", "grp"), P("fsdp", "grp"), P("fsdp", "grp"))
    return jax.shard_map(
        on_device, mesh=mesh, in_specs=in_specs, out_specs=out_specs, check_vma=False
    )
```

time: 200 us -> 70.4 us (0.35)
  blocking collectives: 109 us -> 0 us
  Pallas kernels: 0 us -> 65.2 us
  matrix products: 47.2 us -> 0 us
  waiting for transfers between devices: 18.6 us -> 0 us
  between operations: 14.2 us -> 0.65 us
  other arithmetic: 5.58 us -> 0 us
    all_gather x1 -> x0, blocking collectives: 66.6 us -> none  [on_device(): lax.all_gather(jnp.stack([highest, rescaled, target_logit]), ('grp', 'fsd...]
    pallas_call x0 -> x2, Pallas kernels: none -> 65.2 us  [the longest x1 55.4 us: on_device(): pl.pallas_call(functools.partial(exchange_kernel, n), out_shape=(jax.Shap...]
    dot_general x10 -> x0, matrix products: 47.2 us -> none  [the longest x3 19.1 us: outer(): jnp.einsum('sf,sd->fd', left, right, preferred_element_type=jnp.float32)]
    unnamed x1 -> x0, blocking collectives: 42 us -> none
    all_gather x1 -> x0, waiting for transfers between devices: 18.6 us -> none  [on_device(): lax.all_gather(packed, ('grp', 'fsdp'), axis=0, tiled=True)]
    unnamed x13 -> x7, local copies, waits for them, and re-layouts: 4.66 us -> 4.29 us
  transfers between devices with their start and end apart: 2 -> 0, of which waited for: 1 -> 0; matrix products, arithmetic and copies ran while one was open for 6% -> 0% of each run, Pallas kernels for 0% -> 0%
where the time goes in v1:
time: 70.4 us; the launch traced here: 70.1 us
  Pallas kernels  65.2 us (93%)
  local copies, waits for them, and re-layouts  4.29 us (6%)
    pallas_call x1, Pallas kernels, on_device(): pl.pallas_call(functools.partial(exchange_kernel, n), out_shape=(jax.Shap...  55.4 us
    pallas_call x1, Pallas kernels, on_device(): pl.pallas_call(outer_kernel, grid=(units // tile,), out_shape=(jax.ShapeD...  9.82 us
    unnamed x7, local copies, waits for them, and re-layouts  4.29 us

profile of v1, /device:TPU:0, one launch (start us, length us, event | category | flops | bytes accessed | tf_op | source)
XLA Modules:
  0.0 70.1 jit_solution(3711009079333127131)
XLA Ops:
  0.6 55.4 %shard_map.129 = (f32[1,128]{1,0:T(1,128)}, bf16[3,896,64]{2,1,0:T(8,128)(2,1)}, bf16[64,4096]{1,0:T(8,128)(2,1)}, bf16[64,4096]{1,0:T(8,128)(2,1)}) custom-call(f32[1,4096]{1,0:T(1,128)} %bitcast.4, s32[1,128]{1,0:T(1,128)} %bitcast.5, s32[1,128]{1,0:T(1,128)} %bitcast.6, bf16[128,4096]{1,0:T(8,128)(2,1)} %hidden_hbm.1, bf16[128,8192]{1,0:T(8,128)(2,1)} %input_hbm.1, ...), custom_call_target="tpu_custom_call" | custom-call | tf_op jit(solution)/shard_map/pallas_call | solution.py:350
  56.0 0.0 copy-start
  56.0 1.1 %copy-done = bf16[3,896,64]{2,1,0:T(8,128)(2,1)S(1)} copy-done((bf16[3,896,64]{2,1,0:T(8,128)(2,1)S(1)}, bf16[3,896,64]{2,1,0:T(8,128)(2,1)}, u32[]{:S(2)}) %copy-start) | copy-done | bytes 344088
  57.1 0.0 copy-start.1
  57.1 1.0 %copy-done.1 = bf16[64,4096]{1,0:T(8,128)(2,1)S(1)} copy-done((bf16[64,4096]{1,0:T(8,128)(2,1)S(1)}, bf16[64,4096]{1,0:T(8,128)(2,1)}, u32[]{:S(2)}) %copy-start.1) | copy-done | bytes 524312
  58.1 0.0 copy-start.2
  58.1 1.0 %copy-done.2 = bf16[64,4096]{1,0:T(8,128)(2,1)S(1)} copy-done((bf16[64,4096]{1,0:T(8,128)(2,1)S(1)}, bf16[64,4096]{1,0:T(8,128)(2,1)}, u32[]{:S(2)}) %copy-start.2) | copy-done | bytes 524312
  59.2 9.8 %shard_map.130 = (bf16[896,4096]{1,0:T(8,128)(2,1)}, bf16[896,4096]{1,0:T(8,128)(2,1)}, bf16[896,4096]{1,0:T(8,128)(2,1)}) custom-call(bf16[3,896,64]{2,1,0:T(8,128)(2,1)S(1)} %copy-done, bf16[64,4096]{1,0:T(8,128)(2,1)S(1)} %copy-done.1, bf16[64,4096]{1,0:T(8,128)(2,1)S(1)} %copy-done.2), custom_call_target="tpu_custom_call" | custom-call | tf_op jit(solution)/shard_map/pallas_call | solution.py:401
  69.0 1.1 %copy.15 = f32[128]{0:T(128)} copy(f32[128]{0:T(128)} %bitcast.7) | data formatting | bytes 1024
Async XLA Ops:
  56.0 1.1 %copy-start = (bf16[3,896,64]{2,1,0:T(8,128)(2,1)S(1)}, bf16[3,896,64]{2,1,0:T(8,128)(2,1)}, u32[]{:S(2)}) copy-start(bf16[3,896,64]{2,1,0:T(8,128)(2,1)} %get-tuple-element.12.left_ref) | copy-start | bytes 1032196
  57.1 1.0 %copy-start.1 = (bf16[64,4096]{1,0:T(8,128)(2,1)S(1)}, bf16[64,4096]{1,0:T(8,128)(2,1)}, u32[]{:S(2)}) copy-start(bf16[64,4096]{1,0:T(8,128)(2,1)} %get-tuple-element.13.x_ref) | copy-start | bytes 1572868
  58.1 1.0 %copy-start.2 = (bf16[64,4096]{1,0:T(8,128)(2,1)S(1)}, bf16[64,4096]{1,0:T(8,128)(2,1)}, u32[]{:S(2)}) copy-start(bf16[64,4096]{1,0:T(8,128)(2,1)} %get-tuple-element.14.u_ref) | copy-start | bytes 1572868

commit v2 on v1

--- a/solution.py
+++ b/solution.py
@@ -83,7 +83,7 @@
             ]
         )
     ]
-    for load in loads:
+    for load in loads[:3]:
         load.start()
 
     barrier = pltpu.get_barrier_semaphore()
@@ -153,7 +153,10 @@
     lane = lax.broadcasted_iota(jnp.int32, (ROWS, 128), 1)
     digits = jnp.where(lane == 0, high, jnp.where(lane == 1, low, 0.0)).astype(BF16)
 
-    loads[0].wait()
+    for load in loads[:3]:
+        load.wait()
+    for load in loads[3:]:
+        load.start()
     halves = [select(hidden_v, h * score_half, score_piece) for h in range(2)]
     square = sum(jnp.sum(v * v, axis=1, keepdims=True) for v in halves)
     square = sum(square[q * SLOTS : (q + 1) * SLOTS] for q in range(QUARTERS))
@@ -169,8 +172,6 @@
             gain = jnp.where(piece_row == q, gain_ref[:, start : start + score_piece], gain)
         block_v[h, :, tail:end] = (halves[h] * scale * gain).astype(BF16)
         block_v[h, :, end:] = digits
-    loads[1].wait()
-    loads[2].wait()
     for h in range(2):
         block_v[h, :, :piece] = select(input_v, h * half, piece).astype(BF16)
         block_v[h, :, piece:tail] = select(cot_v, h * half, piece).astype(BF16)
@@ -228,22 +229,41 @@
         x_ref[:, q * piece : (q + 1) * piece] = take(q, 0, piece).astype(BF16)
         u_ref[:, q * piece : (q + 1) * piece] = take(q, piece, tail).astype(BF16)
 
-    units = weight_v.shape[1]
-    tile = units // 2 if units % 256 == 0 else units
-    for i, rows in enumerate([x_ref, x_ref, u_ref]):
+    def multiply(i, rows):
         loads[3 + i].wait()
-
-        @pl.loop(0, units // tile)
-        def _(j):
-            at_units = pl.ds(pl.multiple_of(j * tile, tile), tile)
-            part_v[i, at_units, :] = lax.dot_general(
-                weight_v[i, at_units, :],
-                rows[...],
-                (((1,), (1,)), ((), ())),
-                preferred_element_type=F32,
-            )
-
+        part_v[i] = lax.dot_general(
+            rows[...], weight_v[i], (((1,), (1,)), ((), ())), preferred_element_type=F32
+        )
         send(part_v.at[i], other_v.at[i], part_sem.at[i], mate)
+
+    def summed(i):
+        arrived(other_v.at[i], part_sem.at[i], mate)
+        return part_v[i] + other_v[i]
+
+    lane = lax.broadcasted_iota(jnp.int32, (slots, 128), 1)
+
+    def pack(stats):
+        return jnp.where(lane == 0, stats[0], jnp.where(lane == 1, stats[1], stats[2]))
+
+    def combine(terms):
+        peak = functools.reduce(jnp.maximum, [t[0] for t in terms])
+        total = sum(t[1] * jnp.exp(t[0] - peak) for t in terms)
+        return peak, total, sum(t[2] for t in terms)
+
+    def split(packed):
+        return packed[:, 0:1], packed[:, 1:2], packed[:, 2:3]
+
+    stat_peers = [mate, x_peer, y_peer]
+
+    def stat_send(i, stats):
+        stat_v[i] = pack(stats)
+        send(stat_v.at[i], stat_in.at[i], stat_sem.at[i], stat_peers[i])
+
+    def stat_join(i, stats):
+        arrived(stat_in.at[i], stat_sem.at[i], stat_peers[i])
+        return combine([stats, split(stat_in[i])])
+
+    multiply(0, x_ref)
 
     loads[6].wait()
     arrived(normed_v.at[1 - core], normed_sem.at[0], mate)
@@ -263,42 +283,26 @@
     peak = jnp.max(logits, axis=1, keepdims=True)
     total = jnp.sum(jnp.exp(logits - peak), axis=1, keepdims=True)
     wanted = jnp.sum(jnp.where(hit, logits, 0.0), axis=1, keepdims=True)
-    lane = lax.broadcasted_iota(jnp.int32, (slots, 128), 1)
-
-    def pack(stats):
-        return jnp.where(lane == 0, stats[0], jnp.where(lane == 1, stats[1], stats[2]))
-
-    def combine(terms):
-        peak = functools.reduce(jnp.maximum, [t[0] for t in terms])
-        total = sum(t[1] * jnp.exp(t[0] - peak) for t in terms)
-        return peak, total, sum(t[2] for t in terms)
-
-    def split(packed):
-        return packed[:, 0:1], packed[:, 1:2], packed[:, 2:3]
-
     stats = (peak, total, wanted)
-
-    def multiply(i):
-        arrived(other_v.at[i], part_sem.at[i], mate)
-        return part_v[i] + other_v[i]
-
-    for i, peer in enumerate([mate, x_peer, y_peer]):
-        stat_v[i] = pack(stats)
-        send(stat_v.at[i], stat_in.at[i], stat_sem.at[i], peer)
-        if i == 0:
-            gate = multiply(0)
-            up = multiply(1)
-            s = jax.nn.sigmoid(gate)
-            act = gate * s
-            left_ref[2] = (act * up).astype(BF16)
-            dhidden = multiply(2)
-            left_ref[0] = (dhidden * up * s * (1.0 + gate * (1.0 - s))).astype(BF16)
-            left_ref[1] = (dhidden * act).astype(BF16)
-        arrived(stat_in.at[i], stat_sem.at[i], peer)
-        stats = combine([stats, split(stat_in[i])])
+    stat_send(0, stats)
+    multiply(1, x_ref)
+    stats = stat_join(0, stats)
+    stat_send(1, stats)
+    multiply(2, u_ref)
+    stats = stat_join(1, stats)
+    stat_send(2, stats)
+    gate = summed(0)
+    up = summed(1)
+    s = jax.nn.sigmoid(gate)
+    act = gate * s
+    left_ref[2] = (act * up).astype(BF16)
+    stats = stat_join(2, stats)
     stat_v[3] = pack(stats)
     for d in range(1, groups):
         send(stat_v.at[3], stat_in.at[2 + d], stat_sem.at[2 + d], z_to[d - 1])
+    dhidden = summed(2)
+    left_ref[0] = (dhidden * up * s * (1.0 + gate * (1.0 - s))).astype(BF16)
+    left_ref[1] = (dhidden * act).astype(BF16)
     terms = [stats]
     for d in range(1, groups):
         source = (core, at(lax.rem(a + groups - d, groups), b, c))
@@ -319,8 +323,11 @@
         width = out.shape[1]
         step = 1024 if width % 1024 == 0 else width
         for k in range(width // step):
-            out[:, k * step : (k + 1) * step] = jnp.dot(
-                left_ref[i], right[:, k * step : (k + 1) * step], preferred_element_type=F32
+            out[:, k * step : (k + 1) * step] = lax.dot_general(
+                left_ref[i],
+                right[:, k * step : (k + 1) * step],
+                (((0,), (0,)), ((), ())),
+                preferred_element_type=F32,
             ).astype(BF16)
 
 
@@ -351,7 +358,7 @@
         functools.partial(exchange_kernel, n),
         out_shape=(
             jax.ShapeDtypeStruct((1, tokens), F32),
-            jax.ShapeDtypeStruct((3, units, slots), BF16),
+            jax.ShapeDtypeStruct((3, slots, units), BF16),
             jax.ShapeDtypeStruct((slots, half), BF16),
             jax.ShapeDtypeStruct((slots, half), BF16),
         ),
@@ -367,8 +374,8 @@
             pltpu.VMEM((ROWS, width), BF16),
             pltpu.VMEM((n, ROWS, width), BF16),
             pltpu.VMEM((2, slots, score // 2), BF16),
-            pltpu.VMEM((3, units, slots), F32),
-            pltpu.VMEM((3, units, slots), F32),
+            pltpu.VMEM((3, slots, units), F32),
+            pltpu.VMEM((3, slots, units), F32),
             pltpu.VMEM((slots, vocab), F32),
             pltpu.VMEM((4, slots, 128), F32),
             pltpu.VMEM((2 + groups, slots, 128), F32),
@@ -402,9 +409,9 @@
         outer_kernel,
         grid=(units // tile,),
         out_shape=(jax.ShapeDtypeStruct((units, half), BF16),) * 3,
-        in_specs=[pl.BlockSpec((3, tile, slots), lambda i: (0, i, 0)), whole, whole],
+        in_specs=[pl.BlockSpec((3, slots, tile), lambda i: (0, 0, i)), whole, whole],
         out_specs=(out,) * 3,
-        compiler_params=pltpu.CompilerParams(vmem_limit_bytes=48 * 2**20),
+        compiler_params=pltpu.CompilerParams(vmem_limit_bytes=60 * 2**20),
     )(left, inputs, upstream)
     return (loss.reshape(tokens),) + tuple(grads)
 

time: 70.4 us -> 61.5 us (0.87)
  Pallas kernels: 65.2 us -> 59.5 us
  local copies, waits for them, and re-layouts: 4.29 us -> 1.17 us
    pallas_call x1, Pallas kernels: 55.4 us -> 49.9 us  [on_device(): pl.pallas_call(functools.partial(exchange_kernel, n), out_shape=(jax.Shap...]
    unnamed x7 -> x1, local copies, waits for them, and re-layouts: 4.29 us -> 1.17 us
where the time goes in v2:
time: 61.5 us; the launch traced here: 61.3 us
  Pallas kernels  59.5 us (97%)
  local copies, waits for them, and re-layouts  1.17 us (2%)
  between operations  0.64 us (1%)
    pallas_call x1, Pallas kernels, on_device(): pl.pallas_call(functools.partial(exchange_kernel, n), out_shape=(jax.Shap...  49.9 us
    pallas_call x1, Pallas kernels, on_device(): pl.pallas_call(outer_kernel, grid=(units // tile,), out_shape=(jax.ShapeD...  9.54 us

profile of v2, /device:TPU:0, one launch (start us, length us, event | category | flops | bytes accessed | tf_op | source)
XLA Modules:
  0.0 61.3 jit_solution(17023395750218898213)
XLA Ops:
  0.6 49.9 %shard_map.129 = (f32[1,128]{1,0:T(1,128)}, bf16[3,64,896]{2,1,0:T(8,128)(2,1)}, bf16[64,4096]{1,0:T(8,128)(2,1)}, bf16[64,4096]{1,0:T(8,128)(2,1)}) custom-call(f32[1,4096]{1,0:T(1,128)} %bitcast.4, s32[1,128]{1,0:T(1,128)} %bitcast.5, s32[1,128]{1,0:T(1,128)} %bitcast.6, bf16[128,4096]{1,0:T(8,128)(2,1)} %hidden_hbm.1, bf16[128,8192]{1,0:T(8,128)(2,1)} %input_hbm.1, ...), custom_call_target="tpu_custom_call" | custom-call | tf_op jit(solution)/shard_map/pallas_call | solution.py:357
  50.6 9.5 %shard_map.130 = (bf16[896,4096]{1,0:T(8,128)(2,1)}, bf16[896,4096]{1,0:T(8,128)(2,1)}, bf16[896,4096]{1,0:T(8,128)(2,1)}) custom-call(bf16[3,64,896]{2,1,0:T(8,128)(2,1)} %get-tuple-element.12.left_ref, bf16[64,4096]{1,0:T(8,128)(2,1)} %get-tuple-element.13.x_ref, bf16[64,4096]{1,0:T(8,128)(2,1)} %get-tuple-element.14.u_ref), custom_call_target="tpu_custom_call" | custom-call | tf_op jit(solution)/shard_map/pallas_call | solution.py:408
  60.1 1.2 %copy.15 = f32[128]{0:T(128)} copy(f32[128]{0:T(128)} %bitcast.7) | data formatting | bytes 1024
